TPU v7x, 256 devices: a whole 4x4x8 slice. The times are simulated.
256 devices in a mesh: dp: 2 (over core), seq: 16 (over z_lo, x), chan: 8 (over y, z_hi).
Axes of the slice: x: 4, y: 4, z: 8 (z_hi: 2, z_lo: 4; z = z_hi * 4 + z_lo), core: 2. Of those that a mesh axis runs over, the one named last changes fastest.
Arguments:
- tokens: bfloat16 [1, 8192, 4096], P(None, ('dp', 'seq'), 'chan'), may hold values from -6 to 6
- w_value: bfloat16 [4096, 4096], P(None, 'chan'), may hold values from -0.09375 to 0.09375
- gate_k: bfloat16 [1, 8192, 4096], P(None, ('dp', 'seq'), 'chan'), may hold values from -5 to 5
- gate_q: bfloat16 [1, 8192, 4096], P(None, ('dp', 'seq'), 'chan'), may hold values from -5 to 5
- filter_weight: float32 [64, 4096], P(None, 'chan'), may hold values from -6 to 6
- decay: float32 [4096], P('chan'), may hold values from 0.5 to 8
- skip_bias: float32 [4096], P('chan'), may hold values from 0.5 to 1.5
- cotangent: bfloat16 [1, 8192, 4096], P(None, ('dp', 'seq'), 'chan'), may hold values from -16 to 16
Outputs:
- mixed: bfloat16 [1, 8192, 4096], P(None, ('dp', 'seq'), 'chan')
- grad_tokens: bfloat16 [1, 8192, 4096], P(None, ('dp', 'seq'), 'chan')
- grad_gate_k: bfloat16 [1, 8192, 4096], P(None, ('dp', 'seq'), 'chan')
- grad_gate_q: bfloat16 [1, 8192, 4096], P(None, ('dp', 'seq'), 'chan')
- grad_filter: float32 [64, 4096], P(None, 'chan')
- grad_bias: float32 [4096], P('chan')
All inputs are finite; a program needn't handle non-finite values.
Results may differ from a plain program's by a relative error of at most 0.012.
Values may be sent and summed in bfloat16 or wider, within the bound.
A program may use at most 128 MiB of HBM per device.

v0:
```python
import math
import jax
import jax.numpy as jnp
import numpy as np
from jax import lax
from jax.sharding import PartitionSpec as P

BF = jnp.bfloat16
F32 = jnp.float32


def tables(block, order):
    pos = np.arange(block, dtype=np.float64)
    harm = 2.0 * np.pi / block * np.arange(1, order + 1, dtype=np.float64)
    half = np.pi / block * (2.0 * np.arange(block // 2, dtype=np.float64) + 1.0)
    even = harm[:, None] * pos[None, :]
    odd = half[:, None] * pos[None, :]
    dft = np.concatenate([np.cos(even), np.sin(even), np.cos(odd), np.sin(odd)])
    cross = np.sin(odd) @ np.cos(even).T
    return (dft.astype(np.float32), cross.astype(np.float32))


def dot(a, b):
    return jnp.dot(a.astype(BF), b.astype(BF), preferred_element_type=F32)


def body(tokens, w_value, gate_k, gate_q, filter_weight, decay, skip_bias, cotangent):
    tok = tokens[0]
    block, width = tok.shape
    groups = lax.axis_size(("dp", "seq"))
    index = lax.axis_index(("dp", "seq"))
    length = block * groups
    order = filter_weight.shape[0]
    scale = 1.0 / math.sqrt(order * length)
    dft_np, cross_np = tables(block, order)
    dft = jnp.asarray(dft_np)
    cross = jnp.asarray(cross_np)
    n_even = 2 * order
    half = block // 2
    values = (
        jnp.dot(
            lax.all_gather(tok, "chan", axis=1, tiled=True), w_value, preferred_element_type=F32
        )
        .astype(BF)
        .astype(F32)
    )
    key = gate_k[0].astype(F32)
    query = gate_q[0].astype(F32)
    inc = cotangent[0].astype(F32)
    mixed_in = key * values
    grad_state = query * inc
    pos = jnp.arange(block, dtype=F32)[:, None] / length
    fade = jnp.exp(-pos * decay[None, :])
    grow = jnp.exp(pos * decay[None, :])
    x_spec = dot(dft, mixed_in * grow)
    g_spec = dot(dft, grad_state * fade)
    weights = filter_weight * scale
    kern_c = jnp.sum(weights, axis=0, keepdims=True)
    kern_s = jnp.dot(cross, weights, precision=lax.Precision.HIGHEST)
    states = jnp.concatenate([x_spec[:n_even], g_spec[:n_even]])
    sub = width // groups
    mine = lax.all_to_all(
        states.reshape(2 * n_even, groups, sub),
        ("dp", "seq"),
        split_axis=1,
        concat_axis=1,
        tiled=True,
    )
    dec = lax.dynamic_slice_in_dim(decay, index * sub, sub, 0)
    ids = jnp.arange(groups)
    gap = (ids[:, None] - ids[None, :]).astype(F32)
    low = jnp.where(
        gap[:, :, None] > 0,
        jnp.exp(-jnp.maximum(gap, 0.0)[:, :, None] * dec * (block / length)),
        0.0,
    )
    carried_x = jnp.einsum("ijc,rjc->ric", low, mine[:n_even], precision=lax.Precision.HIGHEST)
    carried_g = jnp.einsum("jic,rjc->ric", low, mine[n_even:], precision=lax.Precision.HIGHEST)
    back = lax.all_to_all(
        jnp.concatenate([carried_x, carried_g]),
        ("dp", "seq"),
        split_axis=1,
        concat_axis=1,
        tiled=True,
    ).reshape(2 * n_even, width)
    z_x, z_g = (back[:n_even], back[n_even:])
    two = jnp.concatenate([weights, weights])
    xe, ge = (x_spec[:n_even], g_spec[:n_even])
    xc, xs = (x_spec[n_even : n_even + half], x_spec[n_even + half :])
    gc, gs = (g_spec[n_even : n_even + half], g_spec[n_even + half :])
    inv = 1.0 / block
    y_spec = jnp.concatenate(
        [
            two * (z_x + 0.5 * xe),
            inv * (kern_c * xc - kern_s * xs),
            inv * (kern_c * xs + kern_s * xc),
        ]
    )
    p_spec = jnp.concatenate(
        [
            two * (z_g + 0.5 * ge),
            inv * (kern_c * gc + kern_s * gs),
            inv * (kern_c * gs - kern_s * gc),
        ]
    )
    gated_state = fade * dot(dft.T, y_spec) + skip_bias * mixed_in
    grad_in = grow * dot(dft.T, p_spec) + skip_bias * grad_state
    n_c = gc * xc + gs * xs
    n_s = gs * xc - gc * xs
    prod = ge * (z_x + 0.5 * xe)
    part = scale * (
        prod[:order]
        + prod[order:]
        + inv
        * (
            jnp.sum(n_c, axis=0, keepdims=True)
            + jnp.dot(cross.T, n_s, precision=lax.Precision.HIGHEST)
        )
    )
    part_bias = jnp.sum(mixed_in * grad_state, axis=0, keepdims=True)
    sums = lax.psum(jnp.concatenate([part, part_bias]), ("dp", "seq"))
    mixed = (query * gated_state).astype(BF)
    grad_values = (key * grad_in).astype(BF)
    terms = lax.dot_general(
        grad_values, w_value, (((1,), (1,)), ((), ())), preferred_element_type=F32
    )
    grad_tok = lax.psum_scatter(terms, "chan", scatter_dimension=1, tiled=True).astype(BF)
    grad_key = (values * grad_in).astype(BF)
    grad_query = (gated_state * inc).astype(BF)
    return (
        mixed[None],
        grad_tok[None],
        grad_key[None],
        grad_query[None],
        sums[:order],
        sums[order],
    )


def solution(mesh):
    rows = P(None, ("dp", "seq"), "chan")
    cols = P(None, "chan")
    return jax.shard_map(
        body,
        mesh=mesh,
        in_specs=(rows, cols, rows, rows, cols, P("chan"), P("chan"), rows),
        out_specs=(rows, rows, rows, rows, cols, P("chan")),
        check_vma=False,
    )
```

profile of v0, /device:TPU:2, one launch (start us, length us, event | category | flops | bytes accessed | tf_op | source)
XLA Modules:
  0.0 545.9 jit_solution(2549810589941749096)
XLA Ops:
  7.2 0.7 all-gather.3.cloned.1.call-update
  7.9 1.5 fusion.20
  9.5 80.6 %all-gather.3.cloned.1.call-done = bf16[1,256,4096]{2,1,0:T(8,128)(2,1)} async-done(((bf16[1,256,512]{2,1,0:T(8,128)(2,1)}), bf16[1,256,4096]{2,1,0:T(8,128)(2,1)}) %all-gather.3.cloned.1.call-update) | async-done | bytes 2097168 | tf_op jit(solution)/shard_map/all_gather | solution.py:42
  90.1 4.1 fusion.9
  94.7 1.0 copy.27
  95.7 5.7 %all-to-all-start = ((f32[256,32,16]{0,2,1:T(8,128)}), f32[256,32,16]{0,2,1:T(8,128)S(1)}, u32[]{:S(2)}, u32[]{:S(2)}) async-start(f32[256,32,16]{0,2,1:T(8,128)} %bitcast.5), calls=%async_computation | async-start | bytes 1048576 | tf_op jit(solution)/shard_map/all_to_all | solution.py:62
  101.5 14.9 %all-to-all-done = f32[256,32,16]{0,2,1:T(8,128)S(1)} async-done(((f32[256,32,16]{0,2,1:T(8,128)}), f32[256,32,16]{0,2,1:T(8,128)S(1)}, u32[]{:S(2)}, u32[]{:S(2)}) %all-to-all-start) | async-done | bytes 524320 | tf_op jit(solution)/shard_map/all_to_all | solution.py:62
  116.4 0.7 convolution_bitcast_fusion.1
  117.1 0.5 convolution_bitcast_fusion
  117.6 1.1 copy.31
  118.7 5.9 %all-to-all-start.1 = ((f32[256,32,16]{0,2,1:T(8,128)}), f32[256,32,16]{0,2,1:T(8,128)S(1)}, u32[]{:S(2)}, u32[]{:S(2)}) async-start(f32[256,32,16]{0,2,1:T(8,128)} %copy.31), calls=%async_computation.1 | async-start | bytes 1048576 | tf_op jit(solution)/shard_map/all_to_all | solution.py:79
  125.2 14.6 %all-to-all-done.1 = f32[256,32,16]{0,2,1:T(8,128)S(1)} async-done(((f32[256,32,16]{0,2,1:T(8,128)}), f32[256,32,16]{0,2,1:T(8,128)S(1)}, u32[]{:S(2)}, u32[]{:S(2)}) %all-to-all-start.1) | async-done | bytes 524320 | tf_op jit(solution)/shard_map/all_to_all | solution.py:79
  139.7 0.7 fusion.87
  140.5 1.1 copy.33
  142.0 1.1 fusion.48
  143.1 1.1 fusion.46
  145.4 1.3 fusion.22
  146.7 0.7 pad_maximum_fusion.3
  147.5 5.4 fusion.23
  152.9 251.9 %all-reduce.2.cloned.1.call-done = f32[65,512]{1,0:T(8,128)} async-done(((f32[65,512]{1,0:T(8,128)}), f32[65,512]{1,0:T(8,128)}) %all-reduce.2.cloned.1.call-update) | async-done | bytes 133136 | tf_op jit(solution)/shard_map/psum | solution.py:121
  404.8 1.3 slice.85
  406.1 1.6 slice.84
  407.7 130.0 %reduce-scatter.2.cloned.1.call-done = f32[256,512]{1,0:T(8,128)} async-done(((f32[256,4096]{1,0:T(8,128)}), f32[256,512]{1,0:T(8,128)}) %reduce-scatter.2.cloned.1.call-update) | async-done | bytes 524304 | tf_op jit(solution)/shard_map/reduce_scatter | solution.py:127
  537.6 1.8 convert_bitcast_fusion
  (46 shorter events, 2.7 us)
Async XLA Ops:
  7.2 82.9 %all-gather.3.cloned.1.call-start = ((), (), s32[]{:S(2)}) async-start(), calls=%async_computation.5 | async-start | bytes 2359296 | tf_op jit(solution)/shard_map/all_gather | solution.py:42
  9.4 84.7 %copy-start.2 = (bf16[1,256,512]{2,1,0:T(8,128)(2,1)S(1)}, bf16[1,256,512]{2,1,0:T(8,128)(2,1)}, u32[]{:S(2)}) copy-start(bf16[1,256,512]{2,1,0:T(8,128)(2,1)} %param.12) | copy-start | bytes 786436
  9.4 84.7 %copy-start.3 = (bf16[384,256]{1,0:T(8,128)(2,1)S(1)}, bf16[384,256]{1,0:T(8,128)(2,1)}, u32[]{:S(2)}) copy-start(bf16[384,256]{1,0:T(8,128)(2,1)} %constant.40) | copy-start | bytes 589828
  9.5 84.7 %copy-start.9 = (f32[512]{0:T(512)S(1)}, f32[512]{0:T(512)}, u32[]{:S(2)}) copy-start(f32[512]{0:T(512)} %param.15) | copy-start | bytes 6148
  94.6 30.1 %copy-start.4 = (f32[64,512]{1,0:T(8,128)S(1)}, f32[64,512]{1,0:T(8,128)}, u32[]{:S(2)}) copy-start(f32[64,512]{1,0:T(8,128)} %param.14) | copy-start | bytes 393220
  94.6 30.1 %copy-start.7 = (f32[128,64]{1,0:T(8,128)S(1)}, f32[128,64]{1,0:T(8,128)}, u32[]{:S(2)}) copy-start(f32[128,64]{1,0:T(8,128)} %constant.39.clone) | copy-start | bytes 98308
  95.7 20.7 %all-to-all-start = ((f32[256,32,16]{0,2,1:T(8,128)}), f32[256,32,16]{0,2,1:T(8,128)S(1)}, u32[]{:S(2)}, u32[]{:S(2)}) async-start(f32[256,32,16]{0,2,1:T(8,128)} %bitcast.5), calls=%async_computation | async-start | bytes 1048576 | tf_op jit(solution)/shard_map/all_to_all | solution.py:62
  118.7 21.0 %all-to-all-start.1 = ((f32[256,32,16]{0,2,1:T(8,128)}), f32[256,32,16]{0,2,1:T(8,128)S(1)}, u32[]{:S(2)}, u32[]{:S(2)}) async-start(f32[256,32,16]{0,2,1:T(8,128)} %copy.31), calls=%async_computation.1 | async-start | bytes 1048576 | tf_op jit(solution)/shard_map/all_to_all | solution.py:79
  124.7 280.1 %all-reduce.2.cloned.1.call-start = ((), (), s32[]{:S(2)}) async-start(), calls=%async_computation.4 | async-start | bytes 294912 | tf_op jit(solution)/shard_map/psum | solution.py:121
  141.7 2.5 copy-start.6
  141.7 3.0 copy-start.8
  141.7 3.3 copy-start
  141.7 3.3 copy-start.1
  141.7 3.3 copy-start.5
  141.8 3.3 copy-start.10
  147.4 390.2 %reduce-scatter.2.cloned.1.call-start = ((), (), s32[]{:S(2)}) async-start(), calls=%async_computation.3 | async-start | bytes 4718592 | tf_op jit(solution)/shard_map/reduce_scatter | solution.py:127
Sparse Core Ops, SparseCore 0:
  10.5 79.5 all-gather.2
  147.5 257.2 all-reduce.1
  409.6 128.0 reduce-scatter.1
where the time goes:
time: 546 us
  waiting for transfers between devices  493 us (90%)
  matrix products  17.5 us (3%)
  between operations  14.1 us (3%)
  starting transfers between devices  11.7 us (2%)
  local copies, waits for them, and re-layouts  7.12 us (1%)
    psum x1, waiting for transfers between devices, body(): sums = lax.psum(jnp.concatenate([part, part_bias]), ('dp', 'seq'))  252 us
    reduce_scatter x1, waiting for transfers between devices, body(): lax.psum_scatter(terms, 'chan', scatter_dimension=1, tiled=True).astype(BF)  130 us
    all_gather x1, waiting for transfers between devices, body(): lax.all_gather(tok, 'chan', axis=1, tiled=True)  80.6 us
    all_to_all x1, waiting for transfers between devices, body(): lax.all_to_all(states.reshape(2 * n_even, groups, sub), ('dp', 'seq'), sp...  14.9 us
    all_to_all x1, waiting for transfers between devices, body(): lax.all_to_all(jnp.concatenate([carried_x, carried_g]), ('dp', 'seq'), sp...  14.6 us
  transfers between devices with their start and end apart: 5, of which 5 were waited for; matrix products, arithmetic and copies ran while one was open for 2% of the time, Pallas kernels for 0%

commit v1 on v0

--- a/solution.py
+++ b/solution.py
@@ -118,7 +118,7 @@
         )
     )
     part_bias = jnp.sum(mixed_in * grad_state, axis=0, keepdims=True)
-    sums = lax.psum(jnp.concatenate([part, part_bias]), ("dp", "seq"))
+    sums = jnp.sum(lax.all_gather(jnp.concatenate([part, part_bias]), ("dp", "seq")), axis=0)
     mixed = (query * gated_state).astype(BF)
     grad_values = (key * grad_in).astype(BF)
     terms = lax.dot_general(

time: 546 us -> 347 us (0.64)
  waiting for transfers between devices: 493 us -> 292 us
    psum x1 -> x0, waiting for transfers between devices: 252 us -> none  [body(): sums = lax.psum(jnp.concatenate([part, part_bias]), ('dp', 'seq'))]
    all_gather x0 -> x1, waiting for transfers between devices: none -> 54.9 us  [body(): lax.all_gather(jnp.concatenate([part, part_bias]), ('dp', 'seq'))]
  transfers between devices with their start and end apart: 5 -> 5, of which waited for: 5 -> 5; matrix products, arithmetic and copies ran while one was open for 2% -> 3% of each run, Pallas kernels for 0% -> 0%
where the time goes in v1:
time: 347 us; the launch traced here: 346 us
  waiting for transfers between devices  292 us (84%)
  matrix products  17.6 us (5%)
  between operations  14.1 us (4%)
  starting transfers between devices  11.7 us (3%)
  other arithmetic  5.56 us (2%)
  local copies, waits for them, and re-layouts  5.5 us (2%)
    reduce_scatter x1, waiting for transfers between devices, body(): lax.psum_scatter(terms, 'chan', scatter_dimension=1, tiled=True).astype(BF)  126 us
    all_gather x1, waiting for transfers between devices, body(): lax.all_gather(tok, 'chan', axis=1, tiled=True)  80.6 us
    all_gather x1, waiting for transfers between devices, body(): lax.all_gather(jnp.concatenate([part, part_bias]), ('dp', 'seq'))  54.9 us
    all_to_all x1, waiting for transfers between devices, body(): lax.all_to_all(states.reshape(2 * n_even, groups, sub), ('dp', 'seq'), sp...  14.9 us
    all_to_all x1, waiting for transfers between devices, body(): lax.all_to_all(jnp.concatenate([carried_x, carried_g]), ('dp', 'seq'), sp...  14.6 us
  transfers between devices with their start and end apart: 5, of which 5 were waited for; matrix products, arithmetic and copies ran while one was open for 3% of the time, Pallas kernels for 0%

profile of v1, /device:TPU:2, one launch (start us, length us, event | category | flops | bytes accessed | tf_op | source)
XLA Modules:
  0.0 346.4 jit_solution(4098998854612397008)
XLA Ops:
  7.2 0.7 all-gather.6.cloned.1.call-update
  7.9 1.5 fusion.20
  9.5 80.6 %all-gather.6.cloned.1.call-done = bf16[1,256,4096]{2,1,0:T(8,128)(2,1)} async-done(((bf16[1,256,512]{2,1,0:T(8,128)(2,1)}), bf16[1,256,4096]{2,1,0:T(8,128)(2,1)}) %all-gather.6.cloned.1.call-update) | async-done | bytes 2097168 | tf_op jit(solution)/shard_map/all_gather | solution.py:42
  90.1 4.1 %fusion.9 = f32[256,512]{1,0:T(8,128)S(1)} fusion(bf16[4096,512]{1,0:T(8,128)(2,1)} %param.11, bf16[1,256,4096]{2,1,0:T(8,128)(2,1)} %all-gather.6.cloned.1.call-done), kind=kOutput, calls=%fused_computation.11 | convolution fusion | flops 1074003968 | bytes 6815744 | tf_op jit(solution)/shard_map/dot_general | solution.py:41
  94.7 1.0 copy.27
  95.7 5.7 %all-to-all-start = ((f32[256,32,16]{0,2,1:T(8,128)}), f32[256,32,16]{0,2,1:T(8,128)S(1)}, u32[]{:S(2)}, u32[]{:S(2)}) async-start(f32[256,32,16]{0,2,1:T(8,128)} %bitcast.5), calls=%async_computation | async-start | bytes 1048576 | tf_op jit(solution)/shard_map/all_to_all | solution.py:62
  101.5 14.9 %all-to-all-done = f32[256,32,16]{0,2,1:T(8,128)S(1)} async-done(((f32[256,32,16]{0,2,1:T(8,128)}), f32[256,32,16]{0,2,1:T(8,128)S(1)}, u32[]{:S(2)}, u32[]{:S(2)}) %all-to-all-start) | async-done | bytes 524320 | tf_op jit(solution)/shard_map/all_to_all | solution.py:62
  116.4 0.7 convolution_bitcast_fusion.1
  117.6 1.1 copy.31
  118.7 5.9 %all-to-all-start.1 = ((f32[256,32,16]{0,2,1:T(8,128)}), f32[256,32,16]{0,2,1:T(8,128)S(1)}, u32[]{:S(2)}, u32[]{:S(2)}) async-start(f32[256,32,16]{0,2,1:T(8,128)} %copy.31), calls=%async_computation.1 | async-start | bytes 1048576 | tf_op jit(solution)/shard_map/all_to_all | solution.py:79
  125.2 14.6 %all-to-all-done.1 = f32[256,32,16]{0,2,1:T(8,128)S(1)} async-done(((f32[256,32,16]{0,2,1:T(8,128)}), f32[256,32,16]{0,2,1:T(8,128)S(1)}, u32[]{:S(2)}, u32[]{:S(2)}) %all-to-all-start.1) | async-done | bytes 524320 | tf_op jit(solution)/shard_map/all_to_all | solution.py:79
  139.7 0.7 fusion.87
  140.5 1.1 copy.33
  142.0 1.1 fusion.48
  143.1 1.1 fusion.46
  145.4 1.3 fusion.22
  146.7 0.7 maximum_bitcast_fusion
  147.5 5.5 %fusion.23 = f32[256,4096]{1,0:T(8,128)} fusion(bf16[4096,512]{1,0:T(8,128)(2,1)} %param.11, f32[256,512]{1,0:T(8,128)S(1)} %fusion.5, bf16[1,256,512]{2,1,0:T(8,128)(2,1)S(1)} %copy-done.2), kind=kOutput, calls=%fused_computation.39 | convolution fusion | flops 1074135040 | bytes 9175040 | tf_op jit(solution)/shard_map/dot_general | solution.py:124
  153.0 54.9 %all-gather.8.cloned.1.call-done = f32[32,65,512]{2,1,0:T(8,128)} async-done(((f32[1,65,512]{2,1,0:T(8,128)}), f32[32,65,512]{2,1,0:T(8,128)}) %all-gather.8.cloned.1.call-update) | async-done | bytes 4259856 | tf_op jit(solution)/shard_map/all_gather | solution.py:121
  207.9 2.8 reduce_sum.39
  210.6 0.6 slice.85
  211.2 0.7 slice.84
  211.9 126.2 %reduce-scatter.2.cloned.1.call-done = f32[256,512]{1,0:T(8,128)} async-done(((f32[256,4096]{1,0:T(8,128)}), f32[256,512]{1,0:T(8,128)}) %reduce-scatter.2.cloned.1.call-update) | async-done | bytes 524304 | tf_op jit(solution)/shard_map/reduce_scatter | solution.py:127
  338.1 1.8 convert_bitcast_fusion
  (47 shorter events, 3.2 us)
Async XLA Ops:
  7.2 82.9 %all-gather.6.cloned.1.call-start = ((), (), s32[]{:S(2)}) async-start(), calls=%async_computation.4 | async-start | bytes 2359296 | tf_op jit(solution)/shard_map/all_gather | solution.py:42
  9.4 84.7 %copy-start.2 = (bf16[1,256,512]{2,1,0:T(8,128)(2,1)S(1)}, bf16[1,256,512]{2,1,0:T(8,128)(2,1)}, u32[]{:S(2)}) copy-start(bf16[1,256,512]{2,1,0:T(8,128)(2,1)} %param.12) | copy-start | bytes 786436
  9.4 84.7 %copy-start.3 = (bf16[384,256]{1,0:T(8,128)(2,1)S(1)}, bf16[384,256]{1,0:T(8,128)(2,1)}, u32[]{:S(2)}) copy-start(bf16[384,256]{1,0:T(8,128)(2,1)} %constant.40) | copy-start | bytes 589828
  9.5 84.7 %copy-start.9 = (f32[512]{0:T(512)S(1)}, f32[512]{0:T(512)}, u32[]{:S(2)}) copy-start(f32[512]{0:T(512)} %param.15) | copy-start | bytes 6148
  94.6 30.1 %copy-start.4 = (f32[64,512]{1,0:T(8,128)S(1)}, f32[64,512]{1,0:T(8,128)}, u32[]{:S(2)}) copy-start(f32[64,512]{1,0:T(8,128)} %param.14) | copy-start | bytes 393220
  94.6 30.1 %copy-start.7 = (f32[128,64]{1,0:T(8,128)S(1)}, f32[128,64]{1,0:T(8,128)}, u32[]{:S(2)}) copy-start(f32[128,64]{1,0:T(8,128)} %constant.39.clone) | copy-start | bytes 98308
  95.7 20.7 %all-to-all-start = ((f32[256,32,16]{0,2,1:T(8,128)}), f32[256,32,16]{0,2,1:T(8,128)S(1)}, u32[]{:S(2)}, u32[]{:S(2)}) async-start(f32[256,32,16]{0,2,1:T(8,128)} %bitcast.5), calls=%async_computation | async-start | bytes 1048576 | tf_op jit(solution)/shard_map/all_to_all | solution.py:62
  118.7 21.0 %all-to-all-start.1 = ((f32[256,32,16]{0,2,1:T(8,128)}), f32[256,32,16]{0,2,1:T(8,128)S(1)}, u32[]{:S(2)}, u32[]{:S(2)}) async-start(f32[256,32,16]{0,2,1:T(8,128)} %copy.31), calls=%async_computation.1 | async-start | bytes 1048576 | tf_op jit(solution)/shard_map/all_to_all | solution.py:79
  124.7 83.2 %all-gather.8.cloned.1.call-start = ((), (), s32[]{:S(2)}) async-start(), calls=%async_computation.5 | async-start | bytes 4866048 | tf_op jit(solution)/shard_map/all_gather | solution.py:121
  141.7 2.5 copy-start.6
  141.7 3.0 copy-start.8
  141.7 3.3 copy-start
  141.7 3.3 copy-start.1
  141.7 3.3 copy-start.5
  141.8 3.3 copy-start.10
  147.4 190.7 %reduce-scatter.2.cloned.1.call-start = ((), (), s32[]{:S(2)}) async-start(), calls=%async_computation.3 | async-start | bytes 4718592 | tf_op jit(solution)/shard_map/reduce_scatter | solution.py:127
Sparse Core Ops, SparseCore 0:
  10.5 79.5 all-gather.5
  147.5 60.2 all-gather.7
  212.0 126.0 reduce-scatter.1
